TPU v7x, 32 devices: a whole 2x2x4 slice. The times are simulated.
32 devices in a mesh: band: 2 (over y), xy: 16 (over z, x, core).
Axes of the slice: x: 2, y: 2, z: 4, core: 2. Of those that a mesh axis runs over, the one named last changes fastest.
Arguments:
- orbitals: float32 [4, 16, 128, 256], P('band', 'xy'), may hold values from -6 to 6
- energies: float32 [4], P('band'), may hold values from -1.5 to -0.25
- occupation: int32 [4], P('band'), may hold values from 1 to 2
- potential: float32 [16, 128, 256], P('xy'), may hold values from 0.25 to 2
- trials: float32 [4, 16, 128, 256], P(None, 'xy'), may hold values from -8 to 23
Outputs:
- density: float32 [4, 16, 128, 256], P(None, 'xy', 'band')
- response_matrix: float32 [4, 4], replicated
All inputs are finite; a program needn't handle non-finite values.
Results may differ from a plain program's by a relative error of at most 0.0001.
Values sent between devices are 32-bit elements; how exact they have to be, the bound alone decides.
A program may use at most 64 MiB of HBM per device.

v0:
```python
import functools
import math

import jax
import jax.numpy as jnp
from jax import lax
from jax.experimental import pallas as pl
from jax.experimental.pallas import tpu as pltpu
from jax.sharding import PartitionSpec as P

ITERS = 3
REACH = 2
SLABS = 2 * REACH + 1
MID = REACH
EDGE = 8
MIDDLE, PARTNER, NEAR, FAR, PASSED = range(5)
HIGHEST = lax.Precision.HIGHEST


def round_up(value, unit):
    return -(-value // unit) * unit


def reduce_groups(bands, slabs):
    groups = []
    stride = 1
    while stride < slabs:
        size = 4 if (slabs // stride) % 4 == 0 else slabs // stride
        groups.append(("xy", size, stride))
        stride *= size
    if bands > 1:
        groups.append(("band", bands, 1))
    return groups


def kernel(dims, groups, orb_ref, energy_ref, occ_ref, pot_ref, trial_ref, dens_ref, resp_ref,
           psi, tri, psi_out, meta, h, u0, v1, v2, lpsi, a_buf, t_out, t_in,
           part, ca, cb, c0f, cf, e0, e1, e2, reds,
           psi_send, psi_recv, tri_send, tri_recv, meta_send, meta_recv, t_send, t_recv,
           red_send, red_recv):
    bands, slabs, nd, kk, ny, nz = dims
    nb = nd * bands
    ys = ny // bands
    ext = ys + EDGE
    kp, jp = round_up(kk, 8), round_up(nb, 8)
    cells = slabs * ny * nz
    b, p = lax.axis_index("band"), lax.axis_index("xy")

    out = 2 * lax.rem(p, 2) - 1

    def at_band(r):
        return lax.rem(b + (r + bands), bands)

    def at_slab(d):
        return lax.rem(p + (d + slabs), slabs)

    def group_rank(g):
        axis, size, stride = groups[g]
        return lax.rem((p if axis == "xy" else b) // stride, size)

    def group_peer(g, q):
        axis, size, stride = groups[g]
        rank = group_rank(g)
        step = (lax.rem(rank + q, size) - rank) * stride
        return {"band": b, "xy": p + step} if axis == "xy" else {"band": b + step, "xy": p}

    barrier = pltpu.get_barrier_semaphore()
    count = 0
    for d in range(-REACH, REACH + 1):
        for r in range(bands):
            if d or r:
                pl.semaphore_signal(barrier, inc=1, device_id={"band": at_band(r), "xy": at_slab(d)},
                                    device_id_type=pl.DeviceIdType.MESH)
                count += 1
    for g, (axis, size, stride) in enumerate(groups):
        for q in range(1, size):
            pl.semaphore_signal(barrier, inc=1, device_id=group_peer(g, q),
                                device_id_type=pl.DeviceIdType.MESH)
            count += 1

    def fill(dst, row_band, src):
        first = pl.multiple_of(row_band * ys, 8)
        low = pl.multiple_of(lax.rem(first + (ny - EDGE), ny), 8)
        high = pl.multiple_of(lax.rem(first + ys, ny), 8)
        dst[0:ys, :] = src[pl.ds(first, ys), :]
        dst[ys:ext, :] = jnp.where(lax.broadcasted_iota(jnp.int32, (EDGE, nz), 0) < EDGE // 2,
                                   src[pl.ds(high, EDGE), :], src[pl.ds(low, EDGE), :])

    own = pl.ds(b * nd, nd)
    for l in range(nd):
        fill(psi.at[MID, b * nd + l], b, orb_ref.at[l, 0])
        for r in range(1, bands):
            fill(psi_out.at[r, l], at_band(r), orb_ref.at[l, 0])
    for k in range(kk):
        fill(tri.at[MID, k], b, trial_ref.at[k, 0])
    fill(tri.at[MID, kk], b, pot_ref.at[0])
    for l in range(nd):
        meta[b, l:l + 1, :] = jnp.full((1, nz), energy_ref[l], jnp.float32)
        meta[b, 8 + l:9 + l, :] = jnp.full((1, nz), occ_ref[l].astype(jnp.float32), jnp.float32)

    pl.semaphore_wait(barrier, count)

    def remote(src, dst, send, recv, device):
        return pltpu.make_async_remote_copy(src_ref=src, dst_ref=dst, send_sem=send, recv_sem=recv,
                                            device_id=device, device_id_type=pl.DeviceIdType.MESH)

    def meta_copy(r, from_band):
        return remote(meta.at[b], meta.at[from_band], meta_send.at[r], meta_recv.at[r],
                      {"band": at_band(r), "xy": p})

    def place(role):
        return {MIDDLE: (0, MID), PARTNER: (-out, MID + out), NEAR: (out, MID - out),
                FAR: (-2 * out, MID + 2 * out), PASSED: (-out, MID + 2 * out)}[role]

    def psi_copy(role, r, first, count):
        d, slot = place(role)
        if role == PASSED:
            src = psi.at[MID + out, :]
        elif r == 0:
            src = psi.at[MID, own]
        elif role == MIDDLE:
            src = psi_out.at[r]
        else:
            src = psi_out.at[r, :]
        dst = psi.at[slot, pl.ds(first, count)]
        if role != MIDDLE:
            dst = psi.at[slot, pl.ds(first, count)]
        return remote(src, dst, psi_send.at[role, r], psi_recv.at[role, r],
                      {"band": at_band(r), "xy": at_slab(d)})

    def tri_copy(role):
        d, slot = place(role)
        src = tri.at[MID + out if role == PASSED else MID, :]
        return remote(src, tri.at[slot, :], tri_send.at[role], tri_recv.at[role],
                      {"band": b, "xy": at_slab(d)})

    def copies(role):
        if role == PASSED:
            return [psi_copy(role, 0, 0, nb), tri_copy(role)]
        moved = [psi_copy(role, r, b * nd, nd) for r in range(bands) if r or role != MIDDLE]
        return moved if role == MIDDLE else moved + [tri_copy(role)]

    sent = []

    def send(role):
        for copy in copies(role):
            copy.start()
            sent.append(copy)

    def wait(role):
        if role == PASSED:
            for copy in copies(role):
                copy.wait_recv()
            return
        for r in range(bands):
            if r or role != MIDDLE:
                psi_copy(role, r, at_band(-r) * nd, nd).wait_recv()
        if role != MIDDLE:
            tri_copy(role).wait_recv()

    for r in range(1, bands):
        meta_copy(r, b).start()
        sent.append(meta_copy(r, b))
    send(MIDDLE)
    send(PARTNER)
    send(NEAR)

    lanes = lax.broadcasted_iota(jnp.int32, (ext, nz), 1)

    def around(c):
        return (pltpu.roll(c, 1, 0) + pltpu.roll(c, ext - 1, 0)
                + jnp.where(lanes == 0, 0.0, pltpu.roll(c, 1, 1))
                + jnp.where(lanes == nz - 1, 0.0, pltpu.roll(c, nz - 1, 1)))

    core = slice(0, ys)

    def put(row, value):
        folded = jnp.sum(value, axis=0, keepdims=True)
        part[pl.ds(row, 1), :] = sum(folded[:, z:z + 128] for z in range(0, nz, 128))

    def total(which, rows, scale, dst):
        length = round_up(rows, 1024) // 8
        lines = lax.broadcasted_iota(jnp.int32, (8, 128), 0)
        y = jnp.zeros((8, length), jnp.float32)
        for line in range(8):
            y = y + lax.dot_general(jnp.where(lines == line, 1.0, 0.0),
                                    part[line * length:(line + 1) * length, :],
                                    (((1,), (1,)), ((), ())), precision=HIGHEST,
                                    preferred_element_type=jnp.float32)
        for g, (axis, size, stride) in enumerate(groups):
            rank = group_rank(g)
            buf = reds[which * len(groups) + g]
            buf[rank, :, :] = y

            def hop(q, slot):
                return remote(buf.at[rank], buf.at[slot], red_send.at[which, g, q],
                              red_recv.at[which, g, q], group_peer(g, q))

            hops = [hop(q, rank) for q in range(1, size)]
            for copy in hops:
                copy.start()
            for q in range(1, size):
                hop(q, lax.rem(rank + (size - q), size)).wait_recv()
            y = buf[0]
            for slot in range(1, size):
                y = y + buf[slot]
            sent.extend(hops)
        for line in range(8):
            dst[line * length:(line + 1) * length, :] = lax.dot_general(
                y, jnp.where(lines == line, scale, 0.0), (((0,), (0,)), ((), ())),
                precision=HIGHEST, preferred_element_type=jnp.float32)

    def wide(row):
        return jnp.concatenate([row] * (nz // 128), axis=1)

    def energy_row(i):
        return meta[i // nd, pl.ds(i % nd, 1), :]

    def occ_row(i):
        return meta[i // nd, pl.ds(8 + i % nd, 1), :]

    def fill_h(s):
        @pl.loop(0, nb)
        def _(i):
            h[s, i] = 0.5 / (3.0 + tri[s, kk] - energy_row(i))

    for r in range(1, bands):
        meta_copy(r, at_band(-r)).wait_recv()
    wait(MIDDLE)
    fill_h(MID)
    block = nb * nb * kp
    square = nb * nb * jp
    part[...] = jnp.zeros_like(part)

    @pl.loop(0, nb)
    def _(i):
        mine = psi[MID, i, core, :]
        inv = 2.0 * h[MID, i, core, :]

        @pl.loop(0, nb)
        def _(j):
            other = psi[MID, j, core, :]
            pair = mine * other
            for k in range(kk):
                both = pair * tri[MID, k, core, :]
                put((i * nb + j) * kp + k, both)
                put(block + (i * nb + j) * kp + k, both * inv)
            weighted = other * inv
            for m in range(nb):
                put(2 * block + (i * nb + j) * jp + m, weighted * psi[MID, m, core, :])
            put(2 * block + square + i * jp + j, pair)

    size_a = 2 * block + square + nb * jp
    total(0, size_a, 1.0 / cells, ca)
    send(FAR)

    def tile(ref, base, i, j, unit):
        return ref[pl.ds(pl.multiple_of(base + (i * nb + j) * unit, 8), 8), :]

    def apply(ref, base, i, j, vectors):
        return sum(ref[pl.ds(base + (i * nb + j) * jp + m, 1), :] * vectors[m] for m in range(nb))

    def gram(j, vectors):
        base = 2 * block + square + j * jp
        return sum(ca[base + m:base + m + 1, :] * vectors[m] for m in range(nb))

    @pl.loop(0, nb)
    def _(i):
        c0 = [tile(ca, 0, i, j, kp) for j in range(nb)]
        for j in range(nb):
            cf[i, j] = apply(ca, 2 * block, i, j, c0) - tile(ca, block, i, j, kp)
            c0f[i, j] = c0[j]

    def fill_u0(s):
        @pl.loop(0, nb)
        def _(i):
            @pl.loop(0, kk)
            def _(k):
                mine = psi[s, i]
                first = -(tri[s, k] * mine)
                second = jnp.zeros_like(first)
                for j in range(nb):
                    field = psi[s, j]
                    first = first + field * wide(c0f[i, j, pl.ds(k, 1), :])
                    second = second + field * wide(cf[i, j, pl.ds(k, 1), :])
                u0[s, i, k] = 2.0 * h[s, i] * first - second

    fill_u0(MID)
    wait(PARTNER)
    fill_h(MID - out)
    fill_u0(MID - out)
    wait(NEAR)
    send(PASSED)
    fill_h(MID + out)
    fill_u0(MID + out)

    part[...] = jnp.zeros_like(part)

    @pl.loop(0, nb)
    def _(j):
        lpsi[j] = psi[MID - 1, j] + psi[MID + 1, j] + around(psi[MID, j])

    @pl.loop(0, nb)
    def _(i):
        @pl.loop(0, nb)
        def _(j):
            a_buf[i, j] = (h[MID - 1, i] * psi[MID - 1, j] + h[MID + 1, i] * psi[MID + 1, j]
                           + around(h[MID, i] * psi[MID, j]))[core, :]

        @pl.loop(0, nb)
        def _(m):
            seen = h[MID, i, core, :] * lpsi[m, core, :]
            for j in range(nb):
                row = (i * nb + j) * jp + m
                put(3 * block + row, psi[MID, j, core, :] * seen)
                put(3 * block + square + row, a_buf[i, j] * seen)

        @pl.loop(0, kk)
        def _(k):
            v2[i, k] = h[MID, i] * (u0[MID - 1, i, k] + u0[MID + 1, i, k] + around(u0[MID, i, k]))
            first = v2[i, k, core, :]
            for j in range(nb):
                put((i * nb + j) * kp + k, psi[MID, j, core, :] * first)

    wait(FAR)
    fill_h(MID + 2 * out)
    fill_u0(MID + 2 * out)
    wait(PASSED)
    fill_h(MID - 2 * out)
    fill_u0(MID - 2 * out)

    @pl.loop(0, nb)
    def _(i):
        @pl.loop(0, kk)
        def _(k):
            for n, s in enumerate((MID - 1, MID + 1)):
                v1[n] = u0[s, i, k] + h[s, i] * (u0[s - 1, i, k] + u0[s + 1, i, k]
                                                + around(u0[s, i, k]))
            v2[i, k] = h[MID, i] * (v1[0] + v1[1] + around(u0[MID, i, k] + v2[i, k]))
            second = v2[i, k, core, :]
            for j in range(nb):
                row = (i * nb + j) * kp + k
                put(block + row, psi[MID, j, core, :] * second)
                put(2 * block + row, a_buf[i, j] * second)

    size_b = 3 * block + 2 * square
    total(1, size_b, 1.0 / cells, cb)

    @pl.loop(0, nb)
    def _(i):
        once = 3 * block
        twice = 3 * block + square
        start = [cf[i, j] for j in range(nb)]
        mu1 = [tile(cb, 0, i, j, kp) for j in range(nb)]
        b0 = [start[j] - gram(j, start) for j in range(nb)]
        x0 = [b0[j] - mu1[j] for j in range(nb)]
        m1 = [tile(cb, block, i, j, kp) + apply(cb, once, i, j, x0) for j in range(nb)]
        x1 = [b0[j] + mu1[j] + gram(j, x0) - m1[j] for j in range(nb)]
        m2 = [mu1[j] + tile(cb, 2 * block, i, j, kp) + apply(cb, twice, i, j, x0)
              + apply(cb, once, i, j, x1) for j in range(nb)]
        for j in range(nb):
            e0[i, j] = x0[j]
            e1[i, j] = x1[j]
            e2[i, j] = b0[j] + m1[j] + gram(j, x1) - m2[j]

    t_out[...] = jnp.zeros_like(t_out)

    @pl.loop(0, nb)
    def _(i):
        weight = occ_row(i)

        @pl.loop(0, kk)
        def _(k):
            first = jnp.zeros((ext, nz), jnp.float32)
            second = u0[MID, i, k] + v2[i, k]
            for j in range(nb):
                first = first + lpsi[j] * wide(e0[i, j, pl.ds(k, 1), :])
                second = second + psi[MID, j] * wide(e1[i, j, pl.ds(k, 1), :])
            v2[i, k] = second + h[MID, i] * first
            inner = v2[i, k, core, :]
            for n, s in enumerate((MID - 1, MID + 1)):
                t_out[n, k] += weight * psi[s, i, core, :] * h[s, i, core, :] * inner

    def t_copy(n):
        return remote(t_out.at[n], t_in.at[n], t_send.at[n], t_recv.at[n],
                      {"band": b, "xy": at_slab(2 * n - 1)})

    for n in range(2):
        t_copy(n).start()
        sent.append(t_copy(n))

    dens_ref[...] = jnp.zeros_like(dens_ref)

    @pl.loop(0, nb)
    def _(i):
        weight = occ_row(i)

        @pl.loop(0, kk)
        def _(k):
            beside = (h[MID, i] * around(v2[i, k]))[core, :]
            flat = u0[MID, i, k, core, :]
            for j in range(nb):
                flat = flat + psi[MID, j, core, :] * wide(e2[i, j, pl.ds(k, 1), :])
            dens_ref[k, 0] += weight * psi[MID, i, core, :] * (flat + beside)

    part[0:1024, :] = jnp.zeros((1024, 128), jnp.float32)

    @pl.loop(0, kk)
    def _(k):
        for l in range(kk):
            put(l * kp + k, tri[MID, l, core, :] * dens_ref[k, 0]
                + tri[MID - 1, l, core, :] * t_out[0, k] + tri[MID + 1, l, core, :] * t_out[1, k])

    scale = 1.0 / math.sqrt(nb)
    total(2, kk * kp, scale / cells, ca)
    column = lax.broadcasted_iota(jnp.int32, (kp, 128), 1)
    picked = sum(jnp.where(column == l, ca[l * kp:(l + 1) * kp, :], 0.0) for l in range(kk))
    resp_ref[...] = picked[:kk, :kk]
    for n in range(2):
        t_copy(n).wait_recv()

    @pl.loop(0, kk)
    def _(k):
        dens_ref[k, 0] = scale * (dens_ref[k, 0] + t_in[0, k] + t_in[1, k])

    for copy in sent:
        copy.wait_send()


def local(sizes, orbitals, energies, occupation, potential, trials):
    bands, slabs = sizes
    nd, width, ny, nz = orbitals.shape
    kk = trials.shape[0]
    nb = nd * bands
    ys = ny // bands
    ext = ys + EDGE
    kp, jp = round_up(kk, 8), round_up(nb, 8)
    block, square = nb * nb * kp, nb * nb * jp
    rows_a = round_up(2 * block + square + nb * jp, 1024)
    rows_b = round_up(3 * block + 2 * square, 1024)
    rows_c = round_up(kk * kp, 1024)
    groups = reduce_groups(bands, slabs)
    widest = max(size for axis, size, stride in groups)

    def f32(*shape):
        return pltpu.VMEM(shape, jnp.float32)

    dma = pltpu.SemaphoreType.DMA
    scratch = [
        f32(SLABS, nb, ext, nz), f32(SLABS, kk + 1, ext, nz), f32(bands, nd, ext, nz),
        f32(bands, 16, nz), f32(SLABS, nb, ext, nz), f32(SLABS, nb, kk, ext, nz),
        f32(2, ext, nz), f32(nb, kk, ext, nz), f32(nb, ext, nz),
        f32(nb, nb, ys, nz), f32(2, kk, ys, nz), f32(2, kk, ys, nz),
        f32(max(rows_a, rows_b), 128), f32(rows_a, 128), f32(rows_b, 128),
        f32(nb, nb, kp, 128), f32(nb, nb, kp, 128), f32(nb, nb, kp, 128),
        f32(nb, nb, kp, 128), f32(nb, nb, kp, 128),
        [f32(size, 8, rows // 8) for rows in (rows_a, rows_b, rows_c) for axis, size, stride in groups],
        dma((5, bands)), dma((5, bands)), dma((5,)), dma((5,)),
        dma((bands,)), dma((bands,)), dma((2,)), dma((2,)),
        dma((3, len(groups), widest)), dma((3, len(groups), widest)),
    ]
    vmem = pl.BlockSpec(memory_space=pltpu.VMEM)
    smem = pl.BlockSpec(memory_space=pltpu.SMEM)
    return pl.pallas_call(
        functools.partial(kernel, (bands, slabs, nd, kk, ny, nz), groups),
        out_shape=(jax.ShapeDtypeStruct((kk, width, ys, nz), jnp.float32),
                   jax.ShapeDtypeStruct((kk, kk), jnp.float32)),
        in_specs=[vmem, smem, smem, vmem, vmem],
        out_specs=(vmem, vmem),
        scratch_shapes=scratch,
        compiler_params=pltpu.CompilerParams(collective_id=0, has_side_effects=True,
                                             vmem_limit_bytes=56 * 1024 * 1024),
    )(orbitals, energies, occupation, potential, trials)


def solution(mesh):
    in_specs = (
        P("band", "xy", None, None),
        P("band"),
        P("band"),
        P("xy", None, None),
        P(None, "xy", None, None),
    )
    out_specs = (P(None, "xy", "band", None), P())
    sizes = (mesh.shape["band"], mesh.shape["xy"])
    return jax.shard_map(functools.partial(local, sizes), mesh=mesh, in_specs=in_specs,
                         out_specs=out_specs, check_vma=False)
```

profile of v0, /device:TPU:0, one launch (start us, length us, event | category | flops | bytes accessed | tf_op | source)
XLA Modules:
  0.0 80.8 jit_solution(16429440279169051227)
XLA Ops:
  0.6 77.9 %shard_map.68 = (f32[4,1,64,256]{3,2,1,0:T(8,128)}, f32[4,4]{1,0:T(4,128)}) custom-call(f32[2,1,128,256]{3,2,1,0:T(8,128)} %orb_ref.1, f32[2]{0:T(128)} %energy_ref.1, s32[2]{0:T(128)} %occ_ref.1, f32[1,128,256]{2,1,0:T(8,128)} %pot_ref.1, f32[4,1,128,256]{3,2,1,0:T(8,128)} %trial_ref.1), custom_call_target="tpu_custom_call" | custom-call | tf_op jit(solution)/shard_map/pallas_call | solution.py:464
  78.5 0.0 copy-start
  78.5 1.7 %copy.9 = f32[4,1,64,256]{3,2,1,0:T(8,128)} copy(f32[4,1,64,256]{3,2,1,0:T(8,128)} %get-tuple-element.4) | data formatting | bytes 524288
  80.2 0.0 copy-done
  80.2 0.6 copy.10
Async XLA Ops:
  78.5 1.7 %copy-start = (f32[4,4]{1,0:T(4,128)S(1)}, f32[4,4]{1,0:T(4,128)}, u32[]{:S(2)}) copy-start(f32[4,4]{1,0:T(4,128)} %get-tuple-element.5) | copy-start | bytes 196
where the time goes:
time: 80.9 us; the launch traced here: 80.8 us
  Pallas kernels  77.9 us (96%)
  local copies, waits for them, and re-layouts  2.26 us (3%)
    pallas_call x1, Pallas kernels, local(): pl.pallas_call(functools.partial(kernel, (bands, slabs, nd, kk, ny, nz),...  77.9 us
    unnamed x4, local copies, waits for them, and re-layouts  2.26 us

commit v1 on v0

--- a/solution.py
+++ b/solution.py
@@ -26,11 +26,14 @@
     stride = 1
     while stride < slabs:
         size = 4 if (slabs // stride) % 4 == 0 else slabs // stride
-        groups.append(("xy", size, stride))
+        groups.append((1 if groups else bands, size, stride))
         stride *= size
-    if bands > 1:
-        groups.append(("band", bands, 1))
     return groups
+
+
+def message(rows):
+    lines = min(8, -(-rows // 128))
+    return lines, round_up(-(-rows // lines), 128)
 
 
 def kernel(dims, groups, orb_ref, energy_ref, occ_ref, pot_ref, trial_ref, dens_ref, resp_ref,
@@ -54,15 +57,19 @@
     def at_slab(d):
         return lax.rem(p + (d + slabs), slabs)
 
+    def group_size(g):
+        return groups[g][0] * groups[g][1]
+
     def group_rank(g):
-        axis, size, stride = groups[g]
-        return lax.rem((p if axis == "xy" else b) // stride, size)
+        across, size, stride = groups[g]
+        rank = lax.rem(p // stride, size)
+        return rank + b * size if across > 1 else rank
 
     def group_peer(g, q):
-        axis, size, stride = groups[g]
-        rank = group_rank(g)
-        step = (lax.rem(rank + q, size) - rank) * stride
-        return {"band": b, "xy": p + step} if axis == "xy" else {"band": b + step, "xy": p}
+        across, size, stride = groups[g]
+        peer = lax.rem(group_rank(g) + q, group_size(g))
+        step = (lax.rem(peer, size) - lax.rem(p // stride, size)) * stride
+        return {"band": peer // size if across > 1 else b, "xy": p + step}
 
     barrier = pltpu.get_barrier_semaphore()
     count = 0
@@ -72,8 +79,8 @@
                 pl.semaphore_signal(barrier, inc=1, device_id={"band": at_band(r), "xy": at_slab(d)},
                                     device_id_type=pl.DeviceIdType.MESH)
                 count += 1
-    for g, (axis, size, stride) in enumerate(groups):
-        for q in range(1, size):
+    for g in range(len(groups)):
+        for q in range(1, group_size(g)):
             pl.semaphore_signal(barrier, inc=1, device_id=group_peer(g, q),
                                 device_id_type=pl.DeviceIdType.MESH)
             count += 1
@@ -179,16 +186,16 @@
         part[pl.ds(row, 1), :] = sum(folded[:, z:z + 128] for z in range(0, nz, 128))
 
     def total(which, rows, scale, dst):
-        length = round_up(rows, 1024) // 8
+        count, length = message(rows)
         lines = lax.broadcasted_iota(jnp.int32, (8, 128), 0)
         y = jnp.zeros((8, length), jnp.float32)
-        for line in range(8):
+        for line in range(count):
             y = y + lax.dot_general(jnp.where(lines == line, 1.0, 0.0),
                                     part[line * length:(line + 1) * length, :],
                                     (((1,), (1,)), ((), ())), precision=HIGHEST,
                                     preferred_element_type=jnp.float32)
-        for g, (axis, size, stride) in enumerate(groups):
-            rank = group_rank(g)
+        for g in range(len(groups)):
+            rank, size = group_rank(g), group_size(g)
             buf = reds[which * len(groups) + g]
             buf[rank, :, :] = y
 
@@ -205,7 +212,7 @@
             for slot in range(1, size):
                 y = y + buf[slot]
             sent.extend(hops)
-        for line in range(8):
+        for line in range(count):
             dst[line * length:(line + 1) * length, :] = lax.dot_general(
                 y, jnp.where(lines == line, scale, 0.0), (((0,), (0,)), ((), ())),
                 precision=HIGHEST, preferred_element_type=jnp.float32)
@@ -315,7 +322,7 @@
                 put(3 * block + row, psi[MID, j, core, :] * seen)
                 put(3 * block + square + row, a_buf[i, j] * seen)
 
-        @pl.loop(0, kk)
+        @pl.loop(0, kk, unroll=True)
         def _(k):
             v2[i, k] = h[MID, i] * (u0[MID - 1, i, k] + u0[MID + 1, i, k] + around(u0[MID, i, k]))
             first = v2[i, k, core, :]
@@ -331,7 +338,7 @@
 
     @pl.loop(0, nb)
     def _(i):
-        @pl.loop(0, kk)
+        @pl.loop(0, kk, unroll=True)
         def _(k):
             for n, s in enumerate((MID - 1, MID + 1)):
                 v1[n] = u0[s, i, k] + h[s, i] * (u0[s - 1, i, k] + u0[s + 1, i, k]
@@ -369,7 +376,7 @@
     def _(i):
         weight = occ_row(i)
 
-        @pl.loop(0, kk)
+        @pl.loop(0, kk, unroll=True)
         def _(k):
             first = jnp.zeros((ext, nz), jnp.float32)
             second = u0[MID, i, k] + v2[i, k]
@@ -395,7 +402,7 @@
     def _(i):
         weight = occ_row(i)
 
-        @pl.loop(0, kk)
+        @pl.loop(0, kk, unroll=True)
         def _(k):
             beside = (h[MID, i] * around(v2[i, k]))[core, :]
             flat = u0[MID, i, k, core, :]
@@ -403,9 +410,9 @@
                 flat = flat + psi[MID, j, core, :] * wide(e2[i, j, pl.ds(k, 1), :])
             dens_ref[k, 0] += weight * psi[MID, i, core, :] * (flat + beside)
 
-    part[0:1024, :] = jnp.zeros((1024, 128), jnp.float32)
-
-    @pl.loop(0, kk)
+    part[0:128, :] = jnp.zeros((128, 128), jnp.float32)
+
+    @pl.loop(0, kk, unroll=True)
     def _(k):
         for l in range(kk):
             put(l * kp + k, tri[MID, l, core, :] * dens_ref[k, 0]
@@ -419,7 +426,7 @@
     for n in range(2):
         t_copy(n).wait_recv()
 
-    @pl.loop(0, kk)
+    @pl.loop(0, kk, unroll=True)
     def _(k):
         dens_ref[k, 0] = scale * (dens_ref[k, 0] + t_in[0, k] + t_in[1, k])
 
@@ -436,11 +443,12 @@
     ext = ys + EDGE
     kp, jp = round_up(kk, 8), round_up(nb, 8)
     block, square = nb * nb * kp, nb * nb * jp
-    rows_a = round_up(2 * block + square + nb * jp, 1024)
-    rows_b = round_up(3 * block + 2 * square, 1024)
-    rows_c = round_up(kk * kp, 1024)
+    rows_a = 2 * block + square + nb * jp
+    rows_b = 3 * block + 2 * square
+    rows_c = kk * kp
+    padded = [math.prod(message(rows)) for rows in (rows_a, rows_b)]
     groups = reduce_groups(bands, slabs)
-    widest = max(size for axis, size, stride in groups)
+    widest = max(across * size for across, size, stride in groups)
 
     def f32(*shape):
         return pltpu.VMEM(shape, jnp.float32)
@@ -451,10 +459,11 @@
         f32(bands, 16, nz), f32(SLABS, nb, ext, nz), f32(SLABS, nb, kk, ext, nz),
         f32(2, ext, nz), f32(nb, kk, ext, nz), f32(nb, ext, nz),
         f32(nb, nb, ys, nz), f32(2, kk, ys, nz), f32(2, kk, ys, nz),
-        f32(max(rows_a, rows_b), 128), f32(rows_a, 128), f32(rows_b, 128),
+        f32(max(padded), 128), f32(padded[0], 128), f32(padded[1], 128),
         f32(nb, nb, kp, 128), f32(nb, nb, kp, 128), f32(nb, nb, kp, 128),
         f32(nb, nb, kp, 128), f32(nb, nb, kp, 128),
-        [f32(size, 8, rows // 8) for rows in (rows_a, rows_b, rows_c) for axis, size, stride in groups],
+        [f32(across * size, 8, message(rows)[1]) for rows in (rows_a, rows_b, rows_c)
+         for across, size, stride in groups],
         dma((5, bands)), dma((5, bands)), dma((5,)), dma((5,)),
         dma((bands,)), dma((bands,)), dma((2,)), dma((2,)),
         dma((3, len(groups), widest)), dma((3, len(groups), widest)),

time: 80.9 us -> 75.6 us (0.934)
  Pallas kernels: 77.9 us -> 72.5 us
    pallas_call x1, Pallas kernels: 77.9 us -> 72.5 us  [local(): pl.pallas_call(functools.partial(kernel, (bands, slabs, nd, kk, ny, nz),...]
where the time goes in v1:
time: 75.6 us; the launch traced here: 75.4 us
  Pallas kernels  72.5 us (96%)
  local copies, waits for them, and re-layouts  2.26 us (3%)
    pallas_call x1, Pallas kernels, local(): pl.pallas_call(functools.partial(kernel, (bands, slabs, nd, kk, ny, nz),...  72.5 us
    unnamed x4, local copies, waits for them, and re-layouts  2.26 us

profile of v1, /device:TPU:0, one launch (start us, length us, event | category | flops | bytes accessed | tf_op | source)
XLA Modules:
  0.0 75.4 jit_solution(5234003345561284547)
XLA Ops:
  0.6 72.5 %shard_map.68 = (f32[4,1,64,256]{3,2,1,0:T(8,128)}, f32[4,4]{1,0:T(4,128)}) custom-call(f32[2,1,128,256]{3,2,1,0:T(8,128)} %orb_ref.1, f32[2]{0:T(128)} %energy_ref.1, s32[2]{0:T(128)} %occ_ref.1, f32[1,128,256]{2,1,0:T(8,128)} %pot_ref.1, f32[4,1,128,256]{3,2,1,0:T(8,128)} %trial_ref.1), custom_call_target="tpu_custom_call" | custom-call | tf_op jit(solution)/shard_map/pallas_call | solution.py:473
  73.1 0.0 copy-start
  73.2 1.7 %copy.9 = f32[4,1,64,256]{3,2,1,0:T(8,128)} copy(f32[4,1,64,256]{3,2,1,0:T(8,128)} %get-tuple-element.4) | data formatting | bytes 524288
  74.8 0.0 copy-done
  74.8 0.6 copy.10
Async XLA Ops:
  73.1 1.7 %copy-start = (f32[4,4]{1,0:T(4,128)S(1)}, f32[4,4]{1,0:T(4,128)}, u32[]{:S(2)}) copy-start(f32[4,4]{1,0:T(4,128)} %get-tuple-element.5) | copy-start | bytes 196

commit v2 on v1

--- a/solution.py
+++ b/solution.py
@@ -182,8 +182,8 @@
     core = slice(0, ys)
 
     def put(row, value):
-        folded = jnp.sum(value, axis=0, keepdims=True)
-        part[pl.ds(row, 1), :] = sum(folded[:, z:z + 128] for z in range(0, nz, 128))
+        folded = sum(value[:, z:z + 128] for z in range(0, nz, 128))
+        part[pl.ds(row, 1), :] = jnp.sum(folded, axis=0, keepdims=True)
 
     def total(which, rows, scale, dst):
         count, length = message(rows)
@@ -244,7 +244,7 @@
         mine = psi[MID, i, core, :]
         inv = 2.0 * h[MID, i, core, :]
 
-        @pl.loop(0, nb)
+        @pl.loop(0, nb, unroll=min(nb, 2))
         def _(j):
             other = psi[MID, j, core, :]
             pair = mine * other
@@ -278,19 +278,24 @@
             cf[i, j] = apply(ca, 2 * block, i, j, c0) - tile(ca, block, i, j, kp)
             c0f[i, j] = c0[j]
 
+    chunk = 24 if ext % 24 == 0 else 8
+
     def fill_u0(s):
         @pl.loop(0, nb)
         def _(i):
-            @pl.loop(0, kk)
-            def _(k):
-                mine = psi[s, i]
-                first = -(tri[s, k] * mine)
-                second = jnp.zeros_like(first)
-                for j in range(nb):
-                    field = psi[s, j]
-                    first = first + field * wide(c0f[i, j, pl.ds(k, 1), :])
-                    second = second + field * wide(cf[i, j, pl.ds(k, 1), :])
-                u0[s, i, k] = 2.0 * h[s, i] * first - second
+            @pl.loop(0, ext // chunk)
+            def _(c):
+                rows = pl.ds(pl.multiple_of(c * chunk, 8), chunk)
+                mine = psi[s, i, rows, :]
+                inv = 2.0 * h[s, i, rows, :]
+                for k in range(kk):
+                    first = -(tri[s, k, rows, :] * mine)
+                    second = jnp.zeros_like(first)
+                    for j in range(nb):
+                        field = psi[s, j, rows, :]
+                        first = first + field * wide(c0f[i, j, k:k + 1, :])
+                        second = second + field * wide(cf[i, j, k:k + 1, :])
+                    u0[s, i, k, rows, :] = inv * first - second
 
     fill_u0(MID)
     wait(PARTNER)
@@ -309,12 +314,12 @@
 
     @pl.loop(0, nb)
     def _(i):
-        @pl.loop(0, nb)
+        @pl.loop(0, nb, unroll=min(nb, 4))
         def _(j):
             a_buf[i, j] = (h[MID - 1, i] * psi[MID - 1, j] + h[MID + 1, i] * psi[MID + 1, j]
                            + around(h[MID, i] * psi[MID, j]))[core, :]
 
-        @pl.loop(0, nb)
+        @pl.loop(0, nb, unroll=min(nb, 4))
         def _(m):
             seen = h[MID, i, core, :] * lpsi[m, core, :]
             for j in range(nb):
@@ -376,17 +381,22 @@
     def _(i):
         weight = occ_row(i)
 
-        @pl.loop(0, kk, unroll=True)
-        def _(k):
-            first = jnp.zeros((ext, nz), jnp.float32)
-            second = u0[MID, i, k] + v2[i, k]
-            for j in range(nb):
-                first = first + lpsi[j] * wide(e0[i, j, pl.ds(k, 1), :])
-                second = second + psi[MID, j] * wide(e1[i, j, pl.ds(k, 1), :])
-            v2[i, k] = second + h[MID, i] * first
-            inner = v2[i, k, core, :]
-            for n, s in enumerate((MID - 1, MID + 1)):
-                t_out[n, k] += weight * psi[s, i, core, :] * h[s, i, core, :] * inner
+        @pl.loop(0, ext // chunk)
+        def _(c):
+            rows = pl.ds(pl.multiple_of(c * chunk, 8), chunk)
+            half = h[MID, i, rows, :]
+            for k in range(kk):
+                first = jnp.zeros((chunk, nz), jnp.float32)
+                second = u0[MID, i, k, rows, :] + v2[i, k, rows, :]
+                for j in range(nb):
+                    first = first + lpsi[j, rows, :] * wide(e0[i, j, k:k + 1, :])
+                    second = second + psi[MID, j, rows, :] * wide(e1[i, j, k:k + 1, :])
+                v2[i, k, rows, :] = second + half * first
+
+        for n, s in enumerate((MID - 1, MID + 1)):
+            factor = weight * psi[s, i, core, :] * h[s, i, core, :]
+            for k in range(kk):
+                t_out[n, k] += factor * v2[i, k, core, :]
 
     def t_copy(n):
         return remote(t_out.at[n], t_in.at[n], t_send.at[n], t_recv.at[n],

time: 75.6 us -> 75.3 us (level)
  no operation moved by 1% of the time
where the time goes in v2:
time: 75.3 us; the launch traced here: 75.1 us
  Pallas kernels  72.2 us (96%)
  local copies, waits for them, and re-layouts  2.26 us (3%)
    pallas_call x1, Pallas kernels, local(): pl.pallas_call(functools.partial(kernel, (bands, slabs, nd, kk, ny, nz),...  72.2 us
    unnamed x4, local copies, waits for them, and re-layouts  2.26 us

profile of v2, /device:TPU:0, one launch (start us, length us, event | category | flops | bytes accessed | tf_op | source)
XLA Modules:
  0.0 75.1 jit_solution(16642736366311800980)
XLA Ops:
  0.6 72.2 %shard_map.68 = (f32[4,1,64,256]{3,2,1,0:T(8,128)}, f32[4,4]{1,0:T(4,128)}) custom-call(f32[2,1,128,256]{3,2,1,0:T(8,128)} %orb_ref.1, f32[2]{0:T(128)} %energy_ref.1, s32[2]{0:T(128)} %occ_ref.1, f32[1,128,256]{2,1,0:T(8,128)} %pot_ref.1, f32[4,1,128,256]{3,2,1,0:T(8,128)} %trial_ref.1), custom_call_target="tpu_custom_call" | custom-call | tf_op jit(solution)/shard_map/pallas_call | solution.py:483
  72.9 0.0 copy-start
  72.9 1.7 %copy.9 = f32[4,1,64,256]{3,2,1,0:T(8,128)} copy(f32[4,1,64,256]{3,2,1,0:T(8,128)} %get-tuple-element.4) | data formatting | bytes 524288
  74.5 0.0 copy-done
  74.6 0.6 copy.10
Async XLA Ops:
  72.9 1.7 %copy-start = (f32[4,4]{1,0:T(4,128)S(1)}, f32[4,4]{1,0:T(4,128)}, u32[]{:S(2)}) copy-start(f32[4,4]{1,0:T(4,128)} %get-tuple-element.5) | copy-start | bytes 196

commit v3 on v2

--- a/solution.py
+++ b/solution.py
@@ -185,7 +185,7 @@
         folded = sum(value[:, z:z + 128] for z in range(0, nz, 128))
         part[pl.ds(row, 1), :] = jnp.sum(folded, axis=0, keepdims=True)
 
-    def total(which, rows, scale, dst):
+    def total(which, rows, scale, dst, beside=None):
         count, length = message(rows)
         lines = lax.broadcasted_iota(jnp.int32, (8, 128), 0)
         y = jnp.zeros((8, length), jnp.float32)
@@ -206,6 +206,8 @@
             hops = [hop(q, rank) for q in range(1, size)]
             for copy in hops:
                 copy.start()
+            if beside and g == len(groups) - 1:
+                beside()
             for q in range(1, size):
                 hop(q, lax.rem(rank + (size - q), size)).wait_recv()
             y = buf[0]
@@ -258,8 +260,7 @@
             put(2 * block + square + i * jp + j, pair)
 
     size_a = 2 * block + square + nb * jp
-    total(0, size_a, 1.0 / cells, ca)
-    send(FAR)
+    total(0, size_a, 1.0 / cells, ca, lambda: send(FAR))
 
     def tile(ref, base, i, j, unit):
         return ref[pl.ds(pl.multiple_of(base + (i * nb + j) * unit, 8), 8), :]
@@ -438,7 +439,7 @@
 
     @pl.loop(0, kk, unroll=True)
     def _(k):
-        dens_ref[k, 0] = scale * (dens_ref[k, 0] + t_in[0, k] + t_in[1, k])
+        dens_ref[k, 0] += t_in[0, k] + t_in[1, k]
 
     for copy in sent:
         copy.wait_send()
@@ -480,7 +481,7 @@
     ]
     vmem = pl.BlockSpec(memory_space=pltpu.VMEM)
     smem = pl.BlockSpec(memory_space=pltpu.SMEM)
-    return pl.pallas_call(
+    density, response_matrix = pl.pallas_call(
         functools.partial(kernel, (bands, slabs, nd, kk, ny, nz), groups),
         out_shape=(jax.ShapeDtypeStruct((kk, width, ys, nz), jnp.float32),
                    jax.ShapeDtypeStruct((kk, kk), jnp.float32)),
@@ -490,6 +491,7 @@
         compiler_params=pltpu.CompilerParams(collective_id=0, has_side_effects=True,
                                              vmem_limit_bytes=56 * 1024 * 1024),
     )(orbitals, energies, occupation, potential, trials)
+    return density / math.sqrt(nb), response_matrix
 
 
 def solution(mesh):

time: 75.3 us -> 72 us (0.956)
  Pallas kernels: 72.2 us -> 68.9 us
  local copies, waits for them, and re-layouts: 2.26 us -> 0.58 us
  other arithmetic: 0 us -> 1.67 us
    pallas_call x1, Pallas kernels: 72.2 us -> 68.9 us  [local(): pl.pallas_call(functools.partial(kernel, (bands, slabs, nd, kk, ny, nz),...]
    unnamed x4 -> x3, local copies, waits for them, and re-layouts: 2.26 us -> 0.58 us
    div x0 -> x1, other arithmetic: none -> 1.67 us  [local(): return (density / math.sqrt(nb), response_matrix)]
where the time goes in v3:
time: 72 us; the launch traced here: 71.8 us
  Pallas kernels  68.9 us (96%)
  other arithmetic  1.67 us (2%)
    pallas_call x1, Pallas kernels, local(): pl.pallas_call(functools.partial(kernel, (bands, slabs, nd, kk, ny, nz),...  68.9 us
    div x1, other arithmetic, local(): return (density / math.sqrt(nb), response_matrix)  1.67 us

profile of v3, /device:TPU:0, one launch (start us, length us, event | category | flops | bytes accessed | tf_op | source)
XLA Modules:
  0.0 71.8 jit_solution(15806706098823283806)
XLA Ops:
  0.6 68.9 %shard_map.68 = (f32[4,1,64,256]{3,2,1,0:T(8,128)}, f32[4,4]{1,0:T(4,128)}) custom-call(f32[2,1,128,256]{3,2,1,0:T(8,128)} %orb_ref.1, f32[2]{0:T(128)} %energy_ref.1, s32[2]{0:T(128)} %occ_ref.1, f32[1,128,256]{2,1,0:T(8,128)} %pot_ref.1, f32[4,1,128,256]{3,2,1,0:T(8,128)} %trial_ref.1), custom_call_target="tpu_custom_call" | custom-call | tf_op jit(solution)/shard_map/pallas_call | solution.py:484
  69.5 0.0 copy-start
  69.5 1.7 %broadcast_multiply_fusion = f32[4,1,64,256]{3,2,1,0:T(8,128)} fusion(f32[4,1,64,256]{3,2,1,0:T(8,128)} %get-tuple-element.4), kind=kLoop, calls=%fused_computation | loop fusion | flops 65536 | bytes 524288 | tf_op jit(solution)/shard_map/div | solution.py:494
  71.2 0.0 copy-done
  71.2 0.6 copy.8
Async XLA Ops:
  69.5 1.7 %copy-start = (f32[4,4]{1,0:T(4,128)S(1)}, f32[4,4]{1,0:T(4,128)}, u32[]{:S(2)}) copy-start(f32[4,4]{1,0:T(4,128)} %get-tuple-element.9) | copy-start | bytes 196
